TPU v7x, 256 devices: a whole 4x4x8 slice. The times are simulated.
256 devices in a mesh: orb: 32 (over y, z), slab: 8 (over x, core).
Axes of the slice: x: 4, y: 4, z: 8, core: 2. Of those that a mesh axis runs over, the one named last changes fastest.
Arguments:
- orbitals: float32 [2, 4096, 16384], P(None, 'orb', 'slab'), may hold values from -1.5 to 1.5
- offsets: int32 [4096], replicated, may hold values from 0 to 6080, as said below
- pairs: int32 [32, 3], P('orb'), may hold values from 0 to 1, as said below
- kernel: float32 [32, 3, 128, 128], P('orb'), may hold values from -0.6 to 0.6
Outputs:
- gradient: float32 [4096, 16384], P('orb', 'slab')
Inputs may be any that keep to these rules, and one draw needn't show every extreme that they name: offsets[f] lies between 192 * (f // 128) and 192 * (f // 128) + 128; in every block the first function's offset is the low end and the second function's the high end. pairs[A, 1] is 1; the list is symmetric, pairs[A, 1 + k] = pairs[A + k, 1 - k]; entries whose block A + k lies outside 0 to 31 are 0.
All inputs are finite; a program needn't handle non-finite values.
Results may differ from a plain program's by a relative error of at most 0.0003.
Values sent between devices are 32-bit elements; how exact they have to be, the bound alone decides.
A program may use at most 128 MiB of HBM per device.

v0:
```python
import functools
import math

import jax
import jax.numpy as jnp
from jax import lax
from jax.experimental import pallas as pl
from jax.experimental.pallas import tpu as pltpu
from jax.sharding import PartitionSpec as P

BLOCK = 128
PATCH = 256
SPREAD = 128
BSTEP = 192
SEG = 16384
QUARTERS = 4
PLANES_PER_CHUNK = 2
CHUNK_IN = PLANES_PER_CHUNK * PATCH
CHUNK = PLANES_PER_CHUNK * BSTEP
MESH = pl.DeviceIdType.MESH
LEFT, RIGHT = 0, 1
SIDE_SLOT = (0, 2)


def lane_gather(tile, index):
    return jnp.take_along_axis(tile, index, axis=1, mode="promise_in_bounds")


def split_rows(value):
    high = value.astype(jnp.bfloat16)
    low = (value - high.astype(jnp.float32)).astype(jnp.bfloat16)
    return high, low


def fold(square):
    return square[:BLOCK] + square[BLOCK:]


def place(planes, u, lane):
    idx_a = jnp.bitwise_and(lane - u, 127)
    idx_b = jnp.bitwise_and(lane - u + 64, 127)
    x0, x1, y0, y1 = (planes[:, i * 128 : (i + 1) * 128] for i in range(4))
    ax0, ax1, ay0, ay1 = (lane_gather(t, idx_a) for t in (x0, x1, y0, y1))
    bx0, bx1, by0, by1 = (lane_gather(t, idx_b) for t in (x0, x1, y0, y1))
    zero = jnp.zeros_like(x0)
    first = lane < 64
    at_u = lane < u
    over = lane < u + 64
    under = lane < u - 64
    left = (
        jnp.where(at_u, zero, ax0),
        jnp.where(at_u, zero, ay0),
        jnp.where(first, jnp.where(at_u, ax0, ax1), jnp.where(over, by0, by1)),
    )
    right = (
        jnp.where(under, bx0, jnp.where(over, bx1, zero)),
        jnp.where(under, by0, jnp.where(over, by1, zero)),
        jnp.where(
            first, jnp.where(under, bx1, zero), jnp.where(at_u, ay1, zero)
        ),
    )
    return left, right


def pick(left, right, u, lane):
    idx_a = jnp.bitwise_and(lane + u, 127)
    idx_b = jnp.bitwise_and(lane + u + 64, 127)
    l0, l1, l2 = (left[:, i * 128 : (i + 1) * 128] for i in range(3))
    r0, r1, r2 = (right[:, i * 128 : (i + 1) * 128] for i in range(3))
    column = lane + u
    outs = []
    for l_full, r_full, near, far in ((l0, r0, idx_a, idx_b), (l1, r1, idx_b, idx_a)):
        gl = lane_gather(l_full, idx_a)
        gm = lane_gather(l2, near)
        gr = lane_gather(r_full, idx_b)
        ge = lane_gather(r2, far)
        outs.append(jnp.where(column < 128, gl, jnp.where(column < 192, gm, gr)))
        outs.append(jnp.where(column < 64, gm, jnp.where(column < 192, gr, ge)))
    return outs


def body(
    n_orb, n_slab, orb_hbm, off_ref, pairs_ref, ker_ref, out_hbm,
    x_in, own, got, own_b, got_b, shift, hacc, hpart, hin, hsum, mats, total, outv,
    in_sem, send_sem, recv_sem, rs_send, rs_recv, ag_send, ag_recv, out_sem,
):
    me = lax.axis_index("orb")
    mine = lax.axis_index("slab")
    before = lax.rem(me + n_orb - 1, n_orb)
    after = lax.rem(me + 1, n_orb)
    rows = BLOCK // n_slab

    def load(m, q):
        return pltpu.make_async_copy(
            orb_hbm.at[m, :, pl.ds(pl.multiple_of(q * CHUNK_IN, CHUNK_IN), CHUNK_IN)],
            x_in.at[m, q], in_sem.at[m, q],
        )

    def send(m, side, q):
        return pltpu.make_async_remote_copy(
            src_ref=own.at[m, side, q], dst_ref=got.at[m, side, q],
            send_sem=send_sem.at[m, side, q], recv_sem=recv_sem.at[m, side, q],
            device_id=(before if side == LEFT else after, mine), device_id_type=MESH,
        )

    def store_out(q):
        return pltpu.make_async_copy(
            outv.at[q],
            out_hbm.at[:, pl.ds(pl.multiple_of(q * CHUNK_IN, CHUNK_IN), CHUNK_IN)],
            out_sem.at[q],
        )

    for m in (1, 0):
        for q in range(QUARTERS):
            load(m, q).start()

    barrier = pltpu.get_barrier_semaphore()
    pl.semaphore_signal(barrier, inc=1, device_id=(before, mine), device_id_type=MESH)
    pl.semaphore_signal(barrier, inc=1, device_id=(after, mine), device_id_type=MESH)
    for d in range(1, n_slab):
        peer = lax.rem(mine + d, n_slab)
        pl.semaphore_signal(barrier, inc=1, device_id=(me, peer), device_id_type=MESH)

    offset_row = off_ref[pl.ds(me, 1), :] - BSTEP * me
    shift[...] = jnp.transpose(jnp.broadcast_to(offset_row, (BLOCK, BLOCK)))
    lane = lax.broadcasted_iota(jnp.int32, (BLOCK, BLOCK), 1)
    pl.semaphore_wait(barrier, 2 + n_slab - 1)

    def place_chunk(m, q):
        left, right = place(x_in[m, q], shift[...], lane)
        for side, tiles in ((LEFT, left), (RIGHT, right)):
            for i, tile in enumerate(tiles):
                own[m, side, q, :, i * 128 : (i + 1) * 128] = tile

    def split_own(m, q):
        for side in (LEFT, RIGHT):
            high, low = split_rows(own[m, side, q])
            own_b[m, side, q, :BLOCK, :] = high
            own_b[m, side, q, BLOCK:, :] = low

    def first_step(q, carry):
        load(1, q).wait()
        place_chunk(1, q)
        send(1, LEFT, q).start()
        send(1, RIGHT, q).start()
        return carry

    lax.fori_loop(0, QUARTERS, first_step, 0)

    for k in range(3):
        weight = pairs_ref[0, k].astype(jnp.float32)
        high, low = split_rows(ker_ref[0, k] * weight)
        for j in range(2):
            mats[k, 1, :BLOCK, j * BLOCK : (j + 1) * BLOCK] = high
            mats[k, 1, BLOCK:, j * BLOCK : (j + 1) * BLOCK] = low
        hacc[k] = jnp.zeros((2 * BLOCK, 2 * BLOCK), jnp.float32)

    def across(a, b):
        return lax.dot_general(
            a, b, (((1,), (1,)), ((), ())), preferred_element_type=jnp.float32
        )

    def second_step(q, carry):
        load(0, q).wait()
        place_chunk(0, q)
        split_own(1, q)
        split_own(0, q)
        for side in (LEFT, RIGHT):
            hacc[1] += across(own_b[0, side, q], own_b[1, side, q])
        return carry

    lax.fori_loop(0, QUARTERS, second_step, 0)

    def split_got(m, side, q):
        high, low = split_rows(got[m, side, q])
        got_b[m, side, q, :BLOCK, :] = high
        got_b[m, side, q, BLOCK:, :] = low

    def third_step(q, carry):
        for side in (LEFT, RIGHT):
            send(1, side, q).wait_recv()
            send(0, side, q).start()
        for side in (LEFT, RIGHT):
            split_got(1, side, q)
            hacc[2 - 2 * side] += across(own_b[0, 1 - side, q], got_b[1, side, q])
        return carry

    lax.fori_loop(0, QUARTERS, third_step, 0)

    for k in range(3):
        square = fold(hacc[k])
        hpart[k] = square[:, :BLOCK] + square[:, BLOCK:]

    def spread(d):
        peer = lax.rem(mine + d, n_slab)
        return pltpu.make_async_remote_copy(
            src_ref=hpart.at[:, pl.ds(pl.multiple_of(peer * rows, rows), rows), :],
            dst_ref=hin.at[d],
            send_sem=rs_send.at[d], recv_sem=rs_recv.at[d],
            device_id=(me, peer), device_id_type=MESH,
        )

    def share(d):
        peer = lax.rem(mine + d, n_slab)
        here = pl.ds(pl.multiple_of(mine * rows, rows), rows)
        return pltpu.make_async_remote_copy(
            src_ref=hsum.at[:, here, :], dst_ref=hsum.at[:, here, :],
            send_sem=ag_send.at[d], recv_sem=ag_recv.at[d],
            device_id=(me, peer), device_id_type=MESH,
        )

    for d in range(1, n_slab):
        spread(d).start()

    def times(k, m, stack):
        return fold(jnp.dot(mats[k, m], stack, preferred_element_type=jnp.float32))

    def kernel_step(q, carry):
        for side in (LEFT, RIGHT):
            other = 1 - side
            total[side, q] = times(1, 1, own_b[1, side, q]) + times(
                2 * side, 1, got_b[1, other, q]
            )
        return carry

    lax.fori_loop(0, QUARTERS, kernel_step, 0)

    mine_rows = pl.ds(pl.multiple_of(mine * rows, rows), rows)
    piece = hpart[:, mine_rows, :]
    for d in range(1, n_slab):
        spread(d).wait_recv()
        piece += hin[d]
    hsum[:, mine_rows, :] = piece
    for d in range(1, n_slab):
        share(d).start()
    for d in range(1, n_slab):
        share(d).wait_recv()

    volume = 1.0 / math.sqrt(SEG)
    for k in range(3):
        weight = pairs_ref[0, k].astype(jnp.float32)
        high, low = split_rows(hsum[k] * (-volume * weight))
        for j in range(2):
            mats[k, 0, :BLOCK, j * BLOCK : (j + 1) * BLOCK] = high
            mats[k, 0, BLOCK:, j * BLOCK : (j + 1) * BLOCK] = low

    def own_step(q, carry):
        for side in (LEFT, RIGHT):
            total[side, q] += times(1, 0, own_b[0, side, q])
        return carry

    lax.fori_loop(0, QUARTERS, own_step, 0)

    def last_step(q, carry):
        sums = []
        for side in (LEFT, RIGHT):
            send(0, 1 - side, q).wait_recv()
            split_got(0, 1 - side, q)
            sums.append(total[side, q] + times(2 * side, 0, got_b[0, 1 - side, q]))
        for i, tile in enumerate(pick(sums[0], sums[1], shift[...], lane)):
            outv[q, :, i * 128 : (i + 1) * 128] = tile
        store_out(q).start()
        return carry

    lax.fori_loop(0, QUARTERS, last_step, 0)

    for d in range(1, n_slab):
        spread(d).wait_send()
        share(d).wait_send()
    for q in range(QUARTERS):
        for m in range(2):
            for side in (LEFT, RIGHT):
                send(m, side, q).wait_send()
        store_out(q).wait()


def per_device(n_orb, n_slab, orbitals, offsets, pairs, kernel):
    f32, b16 = jnp.float32, jnp.bfloat16
    dma = pltpu.SemaphoreType.DMA
    vmem = pl.BlockSpec(memory_space=pltpu.VMEM)
    return pl.pallas_call(
        functools.partial(body, n_orb, n_slab),
        out_shape=jax.ShapeDtypeStruct((BLOCK, QUARTERS * CHUNK_IN), f32),
        in_specs=[
            pl.BlockSpec(memory_space=pl.ANY), vmem,
            pl.BlockSpec(memory_space=pltpu.SMEM), vmem,
        ],
        out_specs=pl.BlockSpec(memory_space=pl.ANY),
        scratch_shapes=[
            pltpu.VMEM((2, QUARTERS, BLOCK, CHUNK_IN), f32),
            pltpu.VMEM((2, 2, QUARTERS, BLOCK, CHUNK), f32),
            pltpu.VMEM((2, 2, QUARTERS, BLOCK, CHUNK), f32),
            pltpu.VMEM((2, 2, QUARTERS, 2 * BLOCK, CHUNK), b16),
            pltpu.VMEM((2, 2, QUARTERS, 2 * BLOCK, CHUNK), b16),
            pltpu.VMEM((BLOCK, BLOCK), jnp.int32),
            pltpu.VMEM((3, 2 * BLOCK, 2 * BLOCK), f32),
            pltpu.VMEM((3, BLOCK, BLOCK), f32),
            pltpu.VMEM((n_slab, 3, BLOCK // n_slab, BLOCK), f32),
            pltpu.VMEM((3, BLOCK, BLOCK), f32),
            pltpu.VMEM((3, 2, 2 * BLOCK, 2 * BLOCK), b16),
            pltpu.VMEM((2, QUARTERS, BLOCK, CHUNK), f32),
            pltpu.VMEM((QUARTERS, BLOCK, CHUNK_IN), f32),
            dma((2, QUARTERS)), dma((2, 2, QUARTERS)), dma((2, 2, QUARTERS)),
            dma((n_slab,)), dma((n_slab,)), dma((n_slab,)), dma((n_slab,)),
            dma((QUARTERS,)),
        ],
        compiler_params=pltpu.CompilerParams(
            collective_id=0, has_side_effects=True, vmem_limit_bytes=40 * 2**20
        ),
        cost_estimate=pl.CostEstimate(
            flops=2400 * 10**6, bytes_accessed=4 * 2**20, transcendentals=0
        ),
    )(orbitals, offsets.reshape(n_orb, BLOCK), pairs, kernel)


def solution(mesh):
    n_orb, n_slab = mesh.shape["orb"], mesh.shape["slab"]
    placed = (P(None, "orb", "slab"), P(), P("orb", None), P("orb", None, None, None))
    return jax.shard_map(
        functools.partial(per_device, n_orb, n_slab), mesh=mesh, in_specs=placed,
        out_specs=P("orb", "slab"), check_vma=False,
    )
```

profile of v0, /device:TPU:1, one launch (start us, length us, event | category | flops | bytes accessed | tf_op | source)
XLA Modules:
  0.0 54.2 jit_solution(17810277680331530701)
XLA Ops:
  0.0 0.0 copy-start
  0.0 1.6 %copy-done = f32[2,128,2048]{2,1,0:T(8,128)S(1)} copy-done((f32[2,128,2048]{2,1,0:T(8,128)S(1)}, f32[2,128,2048]{2,1,0:T(8,128)}, u32[]{:S(2)}) %copy-start) | copy-done | bytes 2097176
  1.6 0.0 copy-start.1
  1.6 0.9 %copy-done.1 = f32[1,3,128,128]{3,2,1,0:T(8,128)S(1)} copy-done((f32[1,3,128,128]{3,2,1,0:T(8,128)S(1)}, f32[1,3,128,128]{3,2,1,0:T(8,128)}, u32[]{:S(2)}) %copy-start.1) | copy-done | bytes 196632
  2.5 0.0 copy-start.2
  2.5 0.7 %copy-done.2 = s32[4096]{0:T(1024)S(1)} copy-done((s32[4096]{0:T(1024)S(1)}, s32[4096]{0:T(1024)}, u32[]{:S(2)}) %copy-start.2) | copy-done | bytes 16408
  3.2 0.0 copy-start.3
  3.2 0.7 %copy-done.3 = s32[1,3]{1,0:T(1,128)S(1)} copy-done((s32[1,3]{1,0:T(1,128)S(1)}, s32[1,3]{1,0:T(1,128)}, u32[]{:S(2)}) %copy-start.3) | copy-done | bytes 36
  3.9 49.3 %shard_map.46 = f32[128,2048]{1,0:T(8,128)S(1)} custom-call(f32[2,128,2048]{2,1,0:T(8,128)S(1)} %copy-done, s32[32,128]{1,0:T(8,128)S(1)} %bitcast.1, s32[1,3]{1,0:T(1,128)S(1)} %copy-done.3, f32[1,3,128,128]{3,2,1,0:T(8,128)S(1)} %copy-done.1), custom_call_target="tpu_custom_call" | custom-call | flops 2400000000 | bytes 4194304 | tf_op jit(solution)/shard_map/pallas_call | solution.py:281
  53.2 1.0 %copy.6 = f32[128,2048]{1,0:T(8,128)} copy(f32[128,2048]{1,0:T(8,128)S(1)} %shard_map.46) | data formatting | bytes 2097152
Async XLA Ops:
  0.0 1.6 %copy-start = (f32[2,128,2048]{2,1,0:T(8,128)S(1)}, f32[2,128,2048]{2,1,0:T(8,128)}, u32[]{:S(2)}) copy-start(f32[2,128,2048]{2,1,0:T(8,128)} %orb_hbm.1) | copy-start | bytes 6291460
  1.6 0.9 %copy-start.1 = (f32[1,3,128,128]{3,2,1,0:T(8,128)S(1)}, f32[1,3,128,128]{3,2,1,0:T(8,128)}, u32[]{:S(2)}) copy-start(f32[1,3,128,128]{3,2,1,0:T(8,128)} %ker_ref.1) | copy-start | bytes 589828
  2.5 0.7 %copy-start.2 = (s32[4096]{0:T(1024)S(1)}, s32[4096]{0:T(1024)}, u32[]{:S(2)}) copy-start(s32[4096]{0:T(1024)} %param.5) | copy-start | bytes 49156
  3.2 0.7 %copy-start.3 = (s32[1,3]{1,0:T(1,128)S(1)}, s32[1,3]{1,0:T(1,128)}, u32[]{:S(2)}) copy-start(s32[1,3]{1,0:T(1,128)} %pairs_ref.1) | copy-start | bytes 40
where the time goes:
time: 54.4 us; the launch traced here: 54.2 us
  Pallas kernels  49.3 us (91%)
  local copies, waits for them, and re-layouts  4.86 us (9%)
    pallas_call x1, Pallas kernels, per_device(): pl.pallas_call(functools.partial(body, n_orb, n_slab), out_shape=jax.Shap...  49.3 us
    unnamed x9, local copies, waits for them, and re-layouts  4.86 us

commit v1 on v0

--- a/solution.py
+++ b/solution.py
@@ -80,14 +80,16 @@
 
 
 def body(
-    n_orb, n_slab, orb_hbm, off_ref, pairs_ref, ker_ref, out_hbm,
-    x_in, own, got, own_b, got_b, shift, hacc, hpart, hin, hsum, mats, total, outv,
-    in_sem, send_sem, recv_sem, rs_send, rs_recv, ag_send, ag_recv, out_sem,
+    n_orb, n_slab, orb_hbm, off_hbm, pairs_hbm, ker_hbm, out_hbm,
+    off_ref, pairs_ref, ker_ref, x_in, own, got, own_b, got_b, shift, hacc, hpart, hin, hsum, mats, total, outv,
+    in_sem, send_sem, recv_sem, rs_send, rs_recv, ag_send, ag_recv, out_sem, small_sem,
 ):
     me = lax.axis_index("orb")
     mine = lax.axis_index("slab")
-    before = lax.rem(me + n_orb - 1, n_orb)
-    after = lax.rem(me + 1, n_orb)
+    has_before = me > 0
+    has_after = me < n_orb - 1
+    before = jnp.maximum(me - 1, 0)
+    after = jnp.minimum(me + 1, n_orb - 1)
     rows = BLOCK // n_slab
 
     def load(m, q):
@@ -110,21 +112,41 @@
             out_sem.at[q],
         )
 
-    for m in (1, 0):
-        for q in range(QUARTERS):
-            load(m, q).start()
-
+    def if_goes(side, action):
+        pl.when(has_before if side == LEFT else has_after)(action)
+
+    def if_comes(side, action):
+        pl.when(has_after if side == LEFT else has_before)(action)
+
+    small = [
+        pltpu.make_async_copy(src, dst, small_sem.at[i])
+        for i, (src, dst) in enumerate(
+            ((off_hbm, off_ref), (pairs_hbm, pairs_ref), (ker_hbm, ker_ref))
+        )
+    ]
     barrier = pltpu.get_barrier_semaphore()
-    pl.semaphore_signal(barrier, inc=1, device_id=(before, mine), device_id_type=MESH)
-    pl.semaphore_signal(barrier, inc=1, device_id=(after, mine), device_id_type=MESH)
+
+    def greet(device):
+        pl.semaphore_signal(barrier, inc=1, device_id=device, device_id_type=MESH)
+
+    small[0].start()
+    load(1, 0).start()
+    if_goes(LEFT, lambda: greet((before, mine)))
+    if_goes(RIGHT, lambda: greet((after, mine)))
     for d in range(1, n_slab):
         peer = lax.rem(mine + d, n_slab)
-        pl.semaphore_signal(barrier, inc=1, device_id=(me, peer), device_id_type=MESH)
-
+        greet((me, peer))
+    for q in range(1, QUARTERS):
+        load(1, q).start()
+    for q in range(QUARTERS):
+        load(0, q).start()
+    small[1].start()
+    small[2].start()
+
+    small[0].wait()
     offset_row = off_ref[pl.ds(me, 1), :] - BSTEP * me
     shift[...] = jnp.transpose(jnp.broadcast_to(offset_row, (BLOCK, BLOCK)))
     lane = lax.broadcasted_iota(jnp.int32, (BLOCK, BLOCK), 1)
-    pl.semaphore_wait(barrier, 2 + n_slab - 1)
 
     def place_chunk(m, q):
         left, right = place(x_in[m, q], shift[...], lane)
@@ -138,18 +160,47 @@
             own_b[m, side, q, :BLOCK, :] = high
             own_b[m, side, q, BLOCK:, :] = low
 
+    def send_both(m, q):
+        if_goes(LEFT, lambda: send(m, LEFT, q).start())
+        if_goes(RIGHT, lambda: send(m, RIGHT, q).start())
+
+    load(1, 0).wait()
+    place_chunk(1, 0)
+    pl.semaphore_wait(
+        barrier,
+        n_slab - 1 + has_before.astype(jnp.int32) + has_after.astype(jnp.int32),
+    )
+    send_both(1, 0)
+
     def first_step(q, carry):
         load(1, q).wait()
         place_chunk(1, q)
-        send(1, LEFT, q).start()
-        send(1, RIGHT, q).start()
-        return carry
-
-    lax.fori_loop(0, QUARTERS, first_step, 0)
+        send_both(1, q)
+        return carry
+
+    lax.fori_loop(1, QUARTERS, first_step, 0)
+
+    for side in (LEFT, RIGHT):
+
+        @pl.when(jnp.logical_not(has_after if side == LEFT else has_before))
+        def _():
+            def blank(q, carry):
+                for m in range(2):
+                    got[m, side, q] = jnp.zeros((BLOCK, CHUNK), jnp.float32)
+                return carry
+
+            lax.fori_loop(0, QUARTERS, blank, 0)
+
+    small[1].wait()
+    small[2].wait()
+
+    def listed(k):
+        return jnp.broadcast_to(
+            pairs_ref[0:1, k : k + 1].astype(jnp.float32), (BLOCK, BLOCK)
+        )
 
     for k in range(3):
-        weight = pairs_ref[0, k].astype(jnp.float32)
-        high, low = split_rows(ker_ref[0, k] * weight)
+        high, low = split_rows(ker_ref[0, k] * listed(k))
         for j in range(2):
             mats[k, 1, :BLOCK, j * BLOCK : (j + 1) * BLOCK] = high
             mats[k, 1, BLOCK:, j * BLOCK : (j + 1) * BLOCK] = low
@@ -178,8 +229,8 @@
 
     def third_step(q, carry):
         for side in (LEFT, RIGHT):
-            send(1, side, q).wait_recv()
-            send(0, side, q).start()
+            if_comes(side, lambda: send(1, side, q).wait_recv())
+        send_both(0, q)
         for side in (LEFT, RIGHT):
             split_got(1, side, q)
             hacc[2 - 2 * side] += across(own_b[0, 1 - side, q], got_b[1, side, q])
@@ -238,8 +289,7 @@
 
     volume = 1.0 / math.sqrt(SEG)
     for k in range(3):
-        weight = pairs_ref[0, k].astype(jnp.float32)
-        high, low = split_rows(hsum[k] * (-volume * weight))
+        high, low = split_rows(hsum[k] * (-volume * listed(k)))
         for j in range(2):
             mats[k, 0, :BLOCK, j * BLOCK : (j + 1) * BLOCK] = high
             mats[k, 0, BLOCK:, j * BLOCK : (j + 1) * BLOCK] = low
@@ -254,7 +304,7 @@
     def last_step(q, carry):
         sums = []
         for side in (LEFT, RIGHT):
-            send(0, 1 - side, q).wait_recv()
+            if_comes(1 - side, lambda: send(0, 1 - side, q).wait_recv())
             split_got(0, 1 - side, q)
             sums.append(total[side, q] + times(2 * side, 0, got_b[0, 1 - side, q]))
         for i, tile in enumerate(pick(sums[0], sums[1], shift[...], lane)):
@@ -270,23 +320,23 @@
     for q in range(QUARTERS):
         for m in range(2):
             for side in (LEFT, RIGHT):
-                send(m, side, q).wait_send()
+                if_goes(side, lambda: send(m, side, q).wait_send())
         store_out(q).wait()
 
 
 def per_device(n_orb, n_slab, orbitals, offsets, pairs, kernel):
     f32, b16 = jnp.float32, jnp.bfloat16
     dma = pltpu.SemaphoreType.DMA
-    vmem = pl.BlockSpec(memory_space=pltpu.VMEM)
+    hbm = pl.BlockSpec(memory_space=pltpu.HBM)
     return pl.pallas_call(
         functools.partial(body, n_orb, n_slab),
         out_shape=jax.ShapeDtypeStruct((BLOCK, QUARTERS * CHUNK_IN), f32),
-        in_specs=[
-            pl.BlockSpec(memory_space=pl.ANY), vmem,
-            pl.BlockSpec(memory_space=pltpu.SMEM), vmem,
-        ],
-        out_specs=pl.BlockSpec(memory_space=pl.ANY),
+        in_specs=[hbm] * 4,
+        out_specs=hbm,
         scratch_shapes=[
+            pltpu.VMEM((n_orb, BLOCK), jnp.int32),
+            pltpu.VMEM(pairs.shape, jnp.int32),
+            pltpu.VMEM(kernel.shape, f32),
             pltpu.VMEM((2, QUARTERS, BLOCK, CHUNK_IN), f32),
             pltpu.VMEM((2, 2, QUARTERS, BLOCK, CHUNK), f32),
             pltpu.VMEM((2, 2, QUARTERS, BLOCK, CHUNK), f32),
@@ -302,10 +352,10 @@
             pltpu.VMEM((QUARTERS, BLOCK, CHUNK_IN), f32),
             dma((2, QUARTERS)), dma((2, 2, QUARTERS)), dma((2, 2, QUARTERS)),
             dma((n_slab,)), dma((n_slab,)), dma((n_slab,)), dma((n_slab,)),
-            dma((QUARTERS,)),
+            dma((QUARTERS,)), dma((3,)),
         ],
         compiler_params=pltpu.CompilerParams(
-            collective_id=0, has_side_effects=True, vmem_limit_bytes=40 * 2**20
+            collective_id=0, has_side_effects=True, vmem_limit_bytes=60 * 2**20
         ),
         cost_estimate=pl.CostEstimate(
             flops=2400 * 10**6, bytes_accessed=4 * 2**20, transcendentals=0

time: 54.4 us -> 48.3 us (0.89)
  the two profiles are of different devices: /device:TPU:1 before, /device:TPU:25 now
where the time goes in v1:
time: 48.3 us; the launch traced here: 48 us
  Pallas kernels  45.7 us (95%)
  local copies, waits for them, and re-layouts  2.3 us (5%)
    pallas_call x1, Pallas kernels, per_device(): pl.pallas_call(functools.partial(body, n_orb, n_slab), out_shape=jax.Shap...  45.7 us
    unnamed x1, local copies, waits for them, and re-layouts  2.3 us

profile of v1, /device:TPU:25, one launch (start us, length us, event | category | flops | bytes accessed | tf_op | source)
XLA Modules:
  0.0 48.0 jit_solution(1319378383747024928)
XLA Ops:
  0.0 45.7 %shard_map.46 = f32[128,2048]{1,0:T(8,128)} custom-call(f32[2,128,2048]{2,1,0:T(8,128)} %orb_hbm.1, s32[32,128]{1,0:T(8,128)} %bitcast.1, s32[1,3]{1,0:T(1,128)} %pairs_hbm.1, f32[1,3,128,128]{3,2,1,0:T(8,128)} %ker_hbm.1), custom_call_target="tpu_custom_call" | custom-call | flops 2400000000 | bytes 4194304 | tf_op jit(solution)/shard_map/pallas_call | solution.py:331
  45.7 2.3 %copy.6 = f32[128,2048]{1,0:T(8,128)} copy(f32[128,2048]{1,0:T(8,128)} %shard_map.46) | data formatting | bytes 2097152

commit v2 on v1

--- a/solution.py
+++ b/solution.py
@@ -19,7 +19,6 @@
 CHUNK = PLANES_PER_CHUNK * BSTEP
 MESH = pl.DeviceIdType.MESH
 LEFT, RIGHT = 0, 1
-SIDE_SLOT = (0, 2)
 
 
 def lane_gather(tile, index):
@@ -80,9 +79,9 @@
 
 
 def body(
-    n_orb, n_slab, orb_hbm, off_hbm, pairs_hbm, ker_hbm, out_hbm,
-    off_ref, pairs_ref, ker_ref, x_in, own, got, own_b, got_b, shift, hacc, hpart, hin, hsum, mats, total, outv,
-    in_sem, send_sem, recv_sem, rs_send, rs_recv, ag_send, ag_recv, out_sem, small_sem,
+    n_orb, n_slab, orb_hbm, off_hbm, pairs_hbm, ker_hbm, out_ref,
+    off_ref, pairs_ref, ker_ref, x_in, own, got, own_b, got_b, shift, hacc, hpart, hin, hsum, mats, total,
+    in_sem, send_sem, recv_sem, rs_send, rs_recv, ag_send, ag_recv, small_sem,
 ):
     me = lax.axis_index("orb")
     mine = lax.axis_index("slab")
@@ -105,13 +104,6 @@
             device_id=(before if side == LEFT else after, mine), device_id_type=MESH,
         )
 
-    def store_out(q):
-        return pltpu.make_async_copy(
-            outv.at[q],
-            out_hbm.at[:, pl.ds(pl.multiple_of(q * CHUNK_IN, CHUNK_IN), CHUNK_IN)],
-            out_sem.at[q],
-        )
-
     def if_goes(side, action):
         pl.when(has_before if side == LEFT else has_after)(action)
 
@@ -308,8 +300,8 @@
             split_got(0, 1 - side, q)
             sums.append(total[side, q] + times(2 * side, 0, got_b[0, 1 - side, q]))
         for i, tile in enumerate(pick(sums[0], sums[1], shift[...], lane)):
-            outv[q, :, i * 128 : (i + 1) * 128] = tile
-        store_out(q).start()
+            at = pl.multiple_of(q * CHUNK_IN + i * 128, 128)
+            out_ref[:, pl.ds(at, 128)] = tile
         return carry
 
     lax.fori_loop(0, QUARTERS, last_step, 0)
@@ -321,18 +313,21 @@
         for m in range(2):
             for side in (LEFT, RIGHT):
                 if_goes(side, lambda: send(m, side, q).wait_send())
-        store_out(q).wait()
 
 
 def per_device(n_orb, n_slab, orbitals, offsets, pairs, kernel):
     f32, b16 = jnp.float32, jnp.bfloat16
     dma = pltpu.SemaphoreType.DMA
     hbm = pl.BlockSpec(memory_space=pltpu.HBM)
+    operands = [
+        pltpu.with_memory_space_constraint(x, pltpu.HBM)
+        for x in (orbitals, offsets.reshape(n_orb, BLOCK), pairs, kernel)
+    ]
     return pl.pallas_call(
         functools.partial(body, n_orb, n_slab),
-        out_shape=jax.ShapeDtypeStruct((BLOCK, QUARTERS * CHUNK_IN), f32),
+        out_shape=pltpu.VMEM((BLOCK, QUARTERS * CHUNK_IN), f32),
         in_specs=[hbm] * 4,
-        out_specs=hbm,
+        out_specs=pl.BlockSpec(memory_space=pltpu.VMEM),
         scratch_shapes=[
             pltpu.VMEM((n_orb, BLOCK), jnp.int32),
             pltpu.VMEM(pairs.shape, jnp.int32),
@@ -349,18 +344,17 @@
             pltpu.VMEM((3, BLOCK, BLOCK), f32),
             pltpu.VMEM((3, 2, 2 * BLOCK, 2 * BLOCK), b16),
             pltpu.VMEM((2, QUARTERS, BLOCK, CHUNK), f32),
-            pltpu.VMEM((QUARTERS, BLOCK, CHUNK_IN), f32),
             dma((2, QUARTERS)), dma((2, 2, QUARTERS)), dma((2, 2, QUARTERS)),
             dma((n_slab,)), dma((n_slab,)), dma((n_slab,)), dma((n_slab,)),
-            dma((QUARTERS,)), dma((3,)),
+            dma((3,)),
         ],
         compiler_params=pltpu.CompilerParams(
-            collective_id=0, has_side_effects=True, vmem_limit_bytes=60 * 2**20
+            collective_id=0, has_side_effects=True, vmem_limit_bytes=40 * 2**20
         ),
         cost_estimate=pl.CostEstimate(
             flops=2400 * 10**6, bytes_accessed=4 * 2**20, transcendentals=0
         ),
-    )(orbitals, offsets.reshape(n_orb, BLOCK), pairs, kernel)
+    )(*operands)
 
 
 def solution(mesh):

time: 48.3 us -> 46.3 us (0.959)
  local copies, waits for them, and re-layouts: 2.3 us -> 0.97 us
  Pallas kernels: 45.7 us -> 45 us
    unnamed x1, local copies, waits for them, and re-layouts: 2.3 us -> 0.97 us
    pallas_call x1, Pallas kernels: 45.7 us -> 45 us  [per_device(): pl.pallas_call(functools.partial(body, n_orb, n_slab), out_shape=pltpu.VM...]
where the time goes in v2:
time: 46.3 us; the launch traced here: 46 us
  Pallas kernels  45 us (97%)
  local copies, waits for them, and re-layouts  0.97 us (2%)
    pallas_call x1, Pallas kernels, per_device(): pl.pallas_call(functools.partial(body, n_orb, n_slab), out_shape=pltpu.VM...  45 us
    unnamed x1, local copies, waits for them, and re-layouts  0.97 us

profile of v2, /device:TPU:25, one launch (start us, length us, event | category | flops | bytes accessed | tf_op | source)
XLA Modules:
  0.0 46.0 jit_solution(762451486104624244)
XLA Ops:
  0.0 45.0 %shard_map.46 = f32[128,2048]{1,0:T(8,128)S(1)} custom-call(f32[2,128,2048]{2,1,0:T(8,128)} %orb_hbm.1, s32[32,128]{1,0:T(8,128)} %bitcast.1, s32[1,3]{1,0:T(1,128)} %pairs_hbm.1, f32[1,3,128,128]{3,2,1,0:T(8,128)} %ker_hbm.1), custom_call_target="tpu_custom_call" | custom-call | flops 2400000000 | bytes 4194304 | tf_op jit(solution)/shard_map/pallas_call | solution.py:326
  45.0 1.0 %copy.6 = f32[128,2048]{1,0:T(8,128)} copy(f32[128,2048]{1,0:T(8,128)S(1)} %shard_map.46) | data formatting | bytes 2097152

commit v3 on v2

--- a/solution.py
+++ b/solution.py
@@ -19,6 +19,8 @@
 CHUNK = PLANES_PER_CHUNK * BSTEP
 MESH = pl.DeviceIdType.MESH
 LEFT, RIGHT = 0, 1
+ROW = 8
+VIA = QUARTERS - 1
 
 
 def lane_gather(tile, index):
@@ -82,6 +84,7 @@
     n_orb, n_slab, orb_hbm, off_hbm, pairs_hbm, ker_hbm, out_ref,
     off_ref, pairs_ref, ker_ref, x_in, own, got, own_b, got_b, shift, hacc, hpart, hin, hsum, mats, total,
     in_sem, send_sem, recv_sem, rs_send, rs_recv, ag_send, ag_recv, small_sem,
+    held, held_sem, onward_sem, ready_sem,
 ):
     me = lax.axis_index("orb")
     mine = lax.axis_index("slab")
@@ -91,6 +94,46 @@
     after = jnp.minimum(me + 1, n_orb - 1)
     rows = BLOCK // n_slab
 
+    flows = n_orb // ROW - 1
+    last = n_orb - 1
+    flow_end = lax.rem(me, ROW) == ROW - 1
+    is_source = jnp.logical_and(flow_end, me < last)
+    is_relay = me == last
+    is_target = jnp.logical_and(lax.rem(me, ROW) == 0, me > 0)
+    flow = me // ROW
+    far = 1 if flows >= 3 else -1
+    stop = (far + 1) * ROW + ROW - 1 if flows >= 3 else last
+    is_stop = jnp.logical_and(me == stop, stop < last)
+    via = jnp.where(flow == far, stop, last)
+
+    def detour():
+        return pltpu.make_async_remote_copy(
+            src_ref=own.at[0, RIGHT, VIA], dst_ref=held.at[flow],
+            send_sem=send_sem.at[0, RIGHT, VIA], recv_sem=held_sem.at[flow],
+            device_id=(via, mine), device_id_type=MESH,
+        )
+
+    def onward(i):
+        return pltpu.make_async_remote_copy(
+            src_ref=held.at[i], dst_ref=got.at[0, RIGHT, VIA],
+            send_sem=onward_sem.at[i], recv_sem=recv_sem.at[0, RIGHT, VIA],
+            device_id=((i + 1) * ROW, mine), device_id_type=MESH,
+        )
+
+    def second_hop():
+        return pltpu.make_async_remote_copy(
+            src_ref=held.at[far], dst_ref=held.at[far],
+            send_sem=onward_sem.at[far], recv_sem=held_sem.at[far],
+            device_id=(last, mine), device_id_type=MESH,
+        )
+
+    def arrived(i):
+        return pltpu.make_async_remote_copy(
+            src_ref=held.at[i], dst_ref=held.at[i],
+            send_sem=onward_sem.at[i], recv_sem=held_sem.at[i],
+            device_id=(before, mine), device_id_type=MESH,
+        )
+
     def load(m, q):
         return pltpu.make_async_copy(
             orb_hbm.at[m, :, pl.ds(pl.multiple_of(q * CHUNK_IN, CHUNK_IN), CHUNK_IN)],
@@ -125,6 +168,8 @@
     load(1, 0).start()
     if_goes(LEFT, lambda: greet((before, mine)))
     if_goes(RIGHT, lambda: greet((after, mine)))
+    pl.when(is_source)(lambda: greet((via, mine)))
+    pl.when(is_target)(lambda: greet((last, mine)))
     for d in range(1, n_slab):
         peer = lax.rem(mine + d, n_slab)
         greet((me, peer))
@@ -160,8 +205,26 @@
     place_chunk(1, 0)
     pl.semaphore_wait(
         barrier,
-        n_slab - 1 + has_before.astype(jnp.int32) + has_after.astype(jnp.int32),
+        n_slab - 1 + has_before.astype(jnp.int32) + has_after.astype(jnp.int32)
+        + (2 * flows - (far > 0)) * is_relay.astype(jnp.int32)
+        + is_stop.astype(jnp.int32),
     )
+
+    def ready(i):
+        pl.semaphore_signal(
+            ready_sem, inc=1, device_id=(i * ROW + ROW - 1, mine), device_id_type=MESH
+        )
+
+
+    @pl.when(is_relay)
+    def _():
+        for i in range(flows):
+            if i != far:
+                ready(i)
+
+    if far > 0:
+        pl.when(is_stop)(lambda: ready(far))
+
     send_both(1, 0)
 
     def first_step(q, carry):
@@ -214,6 +277,11 @@
 
     lax.fori_loop(0, QUARTERS, second_step, 0)
 
+    @pl.when(is_source)
+    def _():
+        pl.semaphore_wait(ready_sem, 1)
+        detour().start()
+
     def split_got(m, side, q):
         high, low = split_rows(got[m, side, q])
         got_b[m, side, q, :BLOCK, :] = high
@@ -222,7 +290,31 @@
     def third_step(q, carry):
         for side in (LEFT, RIGHT):
             if_comes(side, lambda: send(1, side, q).wait_recv())
-        send_both(0, q)
+        if_goes(LEFT, lambda: send(0, LEFT, q).start())
+        straight = jnp.logical_not(jnp.logical_and(is_source, q == VIA))
+        pl.when(jnp.logical_and(has_after, straight))(
+            lambda: send(0, RIGHT, q).start()
+        )
+
+        @pl.when(jnp.logical_and(is_relay, q == VIA - 1))
+        def _():
+            for i in range(flows):
+                if i != far:
+                    arrived(i).wait_recv()
+                    onward(i).start()
+
+        if far > 0:
+
+            @pl.when(jnp.logical_and(is_stop, q == VIA - 2))
+            def _():
+                arrived(far).wait_recv()
+                second_hop().start()
+
+            @pl.when(jnp.logical_and(is_relay, q == VIA))
+            def _():
+                arrived(far).wait_recv()
+                onward(far).start()
+
         for side in (LEFT, RIGHT):
             split_got(1, side, q)
             hacc[2 - 2 * side] += across(own_b[0, 1 - side, q], got_b[1, side, q])
@@ -305,6 +397,14 @@
         return carry
 
     lax.fori_loop(0, QUARTERS, last_step, 0)
+
+    @pl.when(is_relay)
+    def _():
+        for i in range(flows):
+            onward(i).wait_send()
+
+    if far > 0:
+        pl.when(is_stop)(lambda: second_hop().wait_send())
 
     for d in range(1, n_slab):
         spread(d).wait_send()
@@ -347,6 +447,9 @@
             dma((2, QUARTERS)), dma((2, 2, QUARTERS)), dma((2, 2, QUARTERS)),
             dma((n_slab,)), dma((n_slab,)), dma((n_slab,)), dma((n_slab,)),
             dma((3,)),
+            pltpu.VMEM((n_orb // ROW - 1, BLOCK, CHUNK), f32),
+            dma((n_orb // ROW - 1,)), dma((n_orb // ROW - 1,)),
+            pltpu.SemaphoreType.REGULAR,
         ],
         compiler_params=pltpu.CompilerParams(
             collective_id=0, has_side_effects=True, vmem_limit_bytes=40 * 2**20

time: 46.3 us -> 43.3 us (0.935)
  Pallas kernels: 45 us -> 42.1 us
    pallas_call x1, Pallas kernels: 45 us -> 42.1 us  [per_device(): pl.pallas_call(functools.partial(body, n_orb, n_slab), out_shape=pltpu.VM...]
where the time goes in v3:
time: 43.3 us; the launch traced here: 43.1 us
  Pallas kernels  42.1 us (97%)
  local copies, waits for them, and re-layouts  0.97 us (2%)
    pallas_call x1, Pallas kernels, per_device(): pl.pallas_call(functools.partial(body, n_orb, n_slab), out_shape=pltpu.VM...  42.1 us
    unnamed x1, local copies, waits for them, and re-layouts  0.97 us

profile of v3, /device:TPU:25, one launch (start us, length us, event | category | flops | bytes accessed | tf_op | source)
XLA Modules:
  0.0 43.1 jit_solution(12080902753926659965)
XLA Ops:
  0.0 42.1 %shard_map.46 = f32[128,2048]{1,0:T(8,128)S(1)} custom-call(f32[2,128,2048]{2,1,0:T(8,128)} %orb_hbm.1, s32[32,128]{1,0:T(8,128)} %bitcast.1, s32[1,3]{1,0:T(1,128)} %pairs_hbm.1, f32[1,3,128,128]{3,2,1,0:T(8,128)} %ker_hbm.1), custom_call_target="tpu_custom_call" | custom-call | flops 2400000000 | bytes 4194304 | tf_op jit(solution)/shard_map/pallas_call | solution.py:426
  42.1 1.0 %copy.6 = f32[128,2048]{1,0:T(8,128)} copy(f32[128,2048]{1,0:T(8,128)S(1)} %shard_map.46) | data formatting | bytes 2097152

commit v4 on v3

v4 whole, which is shorter than its diff:
```python
import functools
import math

import jax
import jax.numpy as jnp
from jax import lax
from jax.experimental import pallas as pl
from jax.experimental.pallas import tpu as pltpu
from jax.sharding import PartitionSpec as P

BLOCK = 128
PATCH = 256
SPREAD = 128
BSTEP = 192
SEG = 16384
QUARTERS = 4
PLANES = 2
CHUNK_IN = PLANES * PATCH
TILE = 64
TILES = BSTEP // TILE
CHUNK = PLANES * BSTEP
MOST_ROWS = 88
MESH = pl.DeviceIdType.MESH
LEFT, RIGHT = 0, 1
ROW = 8
VIA = QUARTERS - 1


def lane_gather(tile, index):
    return jnp.take_along_axis(tile, index, axis=1, mode="promise_in_bounds")


def split_rows(value):
    high = value.astype(jnp.bfloat16)
    low = (value - high.astype(jnp.float32)).astype(jnp.bfloat16)
    return high, low


def fold(square):
    return square[:BLOCK] + square[BLOCK:]


def place(planes, u, lane):
    merged = []
    for v in range(2):
        vregs = [planes[:, (2 * x + v) * 128 : (2 * x + v + 1) * 128] for x in range(PLANES)]
        row = []
        for s in range(PLANES):
            turned = [
                lane_gather(vregs[x], jnp.bitwise_and(lane + TILE * (s - x) - u, 127))
                for x in range(PLANES)
            ]
            row.append(jnp.where(lane < TILE, turned[0], turned[1]))
        merged.append(row)
    zero = jnp.zeros_like(merged[0][0])
    within = jnp.bitwise_and(lane, TILE - 1) - u
    left, right = [], []
    for t in range(TILES):
        at = within + TILE * t
        near, far = merged[0][t % 2], merged[1][t % 2]
        left.append(jnp.where(at < 0, zero, jnp.where(at < 128, near, far)))
        at = within + TILE * t + BSTEP
        near, far = merged[0][(t + 1) % 2], merged[1][(t + 1) % 2]
        right.append(jnp.where(at < 128, near, jnp.where(at < 256, far, zero)))
    return left, right


def pick(tiles, u, lane):
    column = lane + u
    outs = []
    for x in range(PLANES):
        index = jnp.bitwise_and(column, TILE - 1) + TILE * x
        turned = [lane_gather(tile, index) for tile in tiles]
        for first in (0, 2):
            value = turned[first + 3]
            for t in range(2, -1, -1):
                value = jnp.where(column < TILE * (t + 1), turned[first + t], value)
            outs.append(value)
    return outs


def pieces(side, most):
    if most == BLOCK:
        return ((0, BLOCK, 0, CHUNK),)
    if side == LEFT:
        return ((0, BLOCK, 128, CHUNK), (0, most, 0, 128))
    return ((0, BLOCK, 0, CHUNK - 128), (BLOCK - most, BLOCK, CHUNK - 128, CHUNK))


def body(
    n_orb, n_slab, most, orb_hbm, off_hbm, pairs_hbm, ker_hbm, out_ref, over_ref,
    off_ref, pairs_ref, ker_ref, x_in, own, got, own_b, got_b, shift, sorted_shift, sorter, hacc, hpart, hin, hsum, mats, total,
    in_sem, send_sem, recv_sem, rs_send, rs_recv, ag_send, ag_recv, small_sem,
    held, held_sem, onward_sem, ready_sem,
):
    me = lax.axis_index("orb")
    mine = lax.axis_index("slab")
    has_before = me > 0
    has_after = me < n_orb - 1
    before = jnp.maximum(me - 1, 0)
    after = jnp.minimum(me + 1, n_orb - 1)
    rows = BLOCK // n_slab

    flows = n_orb // ROW - 1
    last = n_orb - 1
    flow_end = lax.rem(me, ROW) == ROW - 1
    is_source = jnp.logical_and(flow_end, me < last)
    is_relay = me == last
    is_target = jnp.logical_and(lax.rem(me, ROW) == 0, me > 0)
    flow = me // ROW
    far = 1 if flows >= 3 else -1
    stop = (far + 1) * ROW + ROW - 1 if flows >= 3 else last
    is_stop = jnp.logical_and(me == stop, stop < last)
    via = jnp.where(flow == far, stop, last)

    def detour():
        return pltpu.make_async_remote_copy(
            src_ref=own.at[0, RIGHT, VIA], dst_ref=held.at[flow],
            send_sem=send_sem.at[0, RIGHT, VIA, 0], recv_sem=held_sem.at[flow],
            device_id=(via, mine), device_id_type=MESH,
        )

    def onward(i):
        return pltpu.make_async_remote_copy(
            src_ref=held.at[i], dst_ref=got.at[0, RIGHT, VIA],
            send_sem=onward_sem.at[i], recv_sem=recv_sem.at[0, RIGHT, VIA, 0],
            device_id=((i + 1) * ROW, mine), device_id_type=MESH,
        )

    def second_hop():
        return pltpu.make_async_remote_copy(
            src_ref=held.at[far], dst_ref=held.at[far],
            send_sem=onward_sem.at[far], recv_sem=held_sem.at[far],
            device_id=(last, mine), device_id_type=MESH,
        )

    def arrived(i):
        return pltpu.make_async_remote_copy(
            src_ref=held.at[i], dst_ref=held.at[i],
            send_sem=onward_sem.at[i], recv_sem=held_sem.at[i],
            device_id=(before, mine), device_id_type=MESH,
        )

    def load(m, q):
        return pltpu.make_async_copy(
            orb_hbm.at[m, :, pl.ds(pl.multiple_of(q * CHUNK_IN, CHUNK_IN), CHUNK_IN)],
            x_in.at[m, q], in_sem.at[m, q],
        )

    def send(m, side, q):
        copies = []
        for i, (top, bottom, first, end) in enumerate(pieces(side, most)):
            src, dst = (
                ref.at[m, side, q, top:bottom, first:end] for ref in (own, got)
            )
            copies.append(
                pltpu.make_async_remote_copy(
                    src_ref=src, dst_ref=dst,
                    send_sem=send_sem.at[m, side, q, i],
                    recv_sem=recv_sem.at[m, side, q, i],
                    device_id=(before if side == LEFT else after, mine),
                    device_id_type=MESH,
                )
            )
        return copies

    def whole():
        return pltpu.make_async_remote_copy(
            src_ref=own.at[0, RIGHT, VIA], dst_ref=got.at[0, RIGHT, VIA],
            send_sem=send_sem.at[0, RIGHT, VIA, 0],
            recv_sem=recv_sem.at[0, RIGHT, VIA, 0],
            device_id=(before, mine), device_id_type=MESH,
        )

    def start(copies):
        for copy in copies:
            copy.start()

    def take(copies):
        for copy in copies:
            copy.wait_recv()

    def drain(copies):
        for copy in copies:
            copy.wait_send()

    def if_goes(side, action):
        pl.when(has_before if side == LEFT else has_after)(action)

    def if_comes(side, action):
        pl.when(has_after if side == LEFT else has_before)(action)

    small = [
        pltpu.make_async_copy(src, dst, small_sem.at[i])
        for i, (src, dst) in enumerate(
            ((off_hbm, off_ref), (pairs_hbm, pairs_ref), (ker_hbm, ker_ref))
        )
    ]
    barrier = pltpu.get_barrier_semaphore()

    def greet(device):
        pl.semaphore_signal(barrier, inc=1, device_id=device, device_id_type=MESH)

    small[0].start()
    load(1, 0).start()
    if_goes(LEFT, lambda: greet((before, mine)))
    if_goes(RIGHT, lambda: greet((after, mine)))
    pl.when(is_source)(lambda: greet((via, mine)))
    pl.when(is_target)(lambda: greet((last, mine)))
    for d in range(1, n_slab):
        peer = lax.rem(mine + d, n_slab)
        greet((me, peer))
    for q in range(1, QUARTERS):
        load(1, q).start()
    for q in range(QUARTERS):
        load(0, q).start()
    small[1].start()
    small[2].start()

    small[0].wait()
    lane = lax.broadcasted_iota(jnp.int32, (BLOCK, BLOCK), 1)
    line = lax.broadcasted_iota(jnp.int32, (BLOCK, BLOCK), 0)

    def shifts_of(block):
        across_lanes = jnp.broadcast_to(
            off_ref[pl.ds(block, 1), :] - BSTEP * block, (BLOCK, BLOCK)
        )
        return across_lanes, jnp.transpose(across_lanes)

    def sorter_of(across_lanes, down_rows):
        ahead = (down_rows < across_lanes) | ((down_rows == across_lanes) & (line < lane))
        place_of = jnp.sum(ahead.astype(jnp.float32), axis=0, keepdims=True)
        return (place_of == line.astype(jnp.float32)).astype(jnp.float32)

    across_lanes, down_rows = shifts_of(me)
    shift[...] = down_rows
    one_hot = sorter_of(across_lanes, down_rows)
    sorter[1, :, :BLOCK] = one_hot.astype(jnp.bfloat16)
    sorter[1, :, BLOCK:] = one_hot.astype(jnp.bfloat16)
    sorted_rows = jnp.sum(one_hot * across_lanes.astype(jnp.float32), axis=1, keepdims=True)
    sorted_shift[...] = jnp.broadcast_to(sorted_rows, (BLOCK, BLOCK)).astype(jnp.int32)

    def place_chunk(m, q):
        high, low = split_rows(x_in[m, q])
        planes = jnp.dot(
            sorter[1], jnp.concatenate([high, low], axis=0),
            preferred_element_type=jnp.float32,
        )
        left, right = place(planes, sorted_shift[...], lane)
        for side, tiles in ((LEFT, left), (RIGHT, right)):
            for i, tile in enumerate(tiles):
                own[m, side, q, :, i * 128 : (i + 1) * 128] = tile

    def split_own(m, q):
        for side in (LEFT, RIGHT):
            high, low = split_rows(own[m, side, q])
            own_b[m, side, q, :BLOCK, :] = high
            own_b[m, side, q, BLOCK:, :] = low

    def send_both(m, q):
        if_goes(LEFT, lambda: start(send(m, LEFT, q)))
        if_goes(RIGHT, lambda: start(send(m, RIGHT, q)))

    load(1, 0).wait()
    place_chunk(1, 0)
    pl.semaphore_wait(
        barrier,
        n_slab - 1 + has_before.astype(jnp.int32) + has_after.astype(jnp.int32)
        + (2 * flows - (far > 0)) * is_relay.astype(jnp.int32)
        + is_stop.astype(jnp.int32),
    )

    def ready(i):
        pl.semaphore_signal(
            ready_sem, inc=1, device_id=(i * ROW + ROW - 1, mine), device_id_type=MESH
        )


    @pl.when(is_relay)
    def _():
        for i in range(flows):
            if i != far:
                ready(i)

    if far > 0:
        pl.when(is_stop)(lambda: ready(far))

    send_both(1, 0)

    def first_step(q, carry):
        load(1, q).wait()
        place_chunk(1, q)
        send_both(1, q)
        return carry

    lax.fori_loop(1, QUARTERS, first_step, 0)

    def blank(q, carry):
        for side in (LEFT, RIGHT):
            comes = has_after if side == LEFT else has_before

            @pl.when(jnp.logical_not(comes))
            def _():
                for m in range(2):
                    got[m, side, q] = jnp.zeros((BLOCK, CHUNK), jnp.float32)

            if most < BLOCK:

                @pl.when(comes)
                def _():
                    for m in range(2):
                        gap = jnp.zeros((BLOCK - most, 128), jnp.float32)
                        if side == LEFT:
                            got[m, side, q, most:, :128] = gap
                        elif m == 1:
                            got[m, side, q, : BLOCK - most, CHUNK - 128 :] = gap
                        else:

                            @pl.when(jnp.logical_not(is_target & (q == VIA)))
                            def _():
                                got[0, side, q, : BLOCK - most, CHUNK - 128 :] = gap

        return carry

    def other_sorters():
        for k, block in ((0, before), (2, after)):
            sorter[k, :, :BLOCK] = sorter_of(*shifts_of(block)).astype(jnp.bfloat16)

    windows = off_ref[...] - BSTEP * lax.broadcasted_iota(jnp.int32, (n_orb, BLOCK), 0)
    excess = jnp.zeros((n_orb, 1), jnp.float32)
    for inside in (windows < TILE, windows > SPREAD - TILE):
        count = jnp.sum(inside.astype(jnp.float32), axis=1, keepdims=True)
        excess = jnp.maximum(excess, count - most)
    over_ref[...] = jnp.broadcast_to(
        jnp.max(excess, axis=0, keepdims=True), (8, 128)
    ).astype(jnp.int32)

    lax.fori_loop(0, QUARTERS, blank, 0)
    other_sorters()
    small[1].wait()
    small[2].wait()

    def across(a, b):
        return lax.dot_general(
            a, b, (((1,), (1,)), ((), ())), preferred_element_type=jnp.float32
        )

    def listed(k):
        return jnp.broadcast_to(
            pairs_ref[0:1, k : k + 1].astype(jnp.float32), (BLOCK, BLOCK)
        )

    for k in range(3):
        high, low = split_rows(ker_ref[0, k] * listed(k))
        both = across(jnp.concatenate([high, low], axis=0), sorter[k, :, :BLOCK])
        for j in range(2):
            mats[k, 1, :, j * BLOCK : (j + 1) * BLOCK] = both.astype(jnp.bfloat16)
        hacc[k] = jnp.zeros((2 * BLOCK, 2 * BLOCK), jnp.float32)

    def second_step(q, carry):
        load(0, q).wait()
        place_chunk(0, q)
        split_own(1, q)
        split_own(0, q)
        for side in (LEFT, RIGHT):
            hacc[1] += across(own_b[0, side, q], own_b[1, side, q])
        return carry

    lax.fori_loop(0, QUARTERS, second_step, 0)

    slots = ((2, (1,)), (0, (0, 2)))

    def spread(group, d):
        first, ks = slots[group]
        peer = lax.rem(mine + d, n_slab)
        there = pl.ds(pl.multiple_of(peer * rows, rows), rows)
        return pltpu.make_async_remote_copy(
            src_ref=hpart.at[first : first + len(ks), there, :],
            dst_ref=hin.at[d, first : first + len(ks)],
            send_sem=rs_send.at[group, d], recv_sem=rs_recv.at[group, d],
            device_id=(me, peer), device_id_type=MESH,
        )

    def share(group, d):
        first, ks = slots[group]
        peer = lax.rem(mine + d, n_slab)
        here = pl.ds(pl.multiple_of(mine * rows, rows), rows)
        part = hsum.at[first : first + len(ks), here, :]
        return pltpu.make_async_remote_copy(
            src_ref=part, dst_ref=part,
            send_sem=ag_send.at[group, d], recv_sem=ag_recv.at[group, d],
            device_id=(me, peer), device_id_type=MESH,
        )

    def reduce_terms(group):
        first, ks = slots[group]
        for i, k in enumerate(ks):
            square = fold(hacc[k])
            hpart[first + i] = square[:, :BLOCK] + square[:, BLOCK:]
        for d in range(1, n_slab):
            spread(group, d).start()

    def reduce_sums(group):
        first, ks = slots[group]
        mine_rows = pl.ds(pl.multiple_of(mine * rows, rows), rows)
        piece = hpart[first : first + len(ks), mine_rows, :]
        for d in range(1, n_slab):
            spread(group, d).wait_recv()
            piece += hin[d, first : first + len(ks)]
        hsum[first : first + len(ks), mine_rows, :] = piece
        for d in range(1, n_slab):
            share(group, d).start()

    volume = 1.0 / math.sqrt(SEG)

    def finish_sums(group):
        first, ks = slots[group]
        for d in range(1, n_slab):
            share(group, d).wait_recv()
        for i, k in enumerate(ks):
            high, low = split_rows(hsum[first + i] * (-volume * listed(k)))
            both = lax.dot_general(
                sorter[1, :, :BLOCK], jnp.concatenate([high, low], axis=1),
                (((0,), (0,)), ((), ())), preferred_element_type=jnp.float32,
            ).astype(jnp.bfloat16)
            for j in range(2):
                mats[k, 0, :BLOCK, j * BLOCK : (j + 1) * BLOCK] = both[:, :BLOCK]
                mats[k, 0, BLOCK:, j * BLOCK : (j + 1) * BLOCK] = both[:, BLOCK:]

    def times(k, m, stack):
        return fold(jnp.dot(mats[k, m], stack, preferred_element_type=jnp.float32))

    reduce_terms(0)

    @pl.when(is_source)
    def _():
        pl.semaphore_wait(ready_sem, 1)
        detour().start()

    def split_got(m, side, q):
        high, low = split_rows(got[m, side, q])
        got_b[m, side, q, :BLOCK, :] = high
        got_b[m, side, q, BLOCK:, :] = low

    def third_step(q, carry):
        for side in (LEFT, RIGHT):
            if_comes(side, lambda: take(send(1, side, q)))
        if_goes(LEFT, lambda: start(send(0, LEFT, q)))
        straight = jnp.logical_not(jnp.logical_and(is_source, q == VIA))
        pl.when(jnp.logical_and(has_after, straight))(
            lambda: start(send(0, RIGHT, q))
        )

        @pl.when(jnp.logical_and(is_relay, q == VIA - 1))
        def _():
            for i in range(flows):
                if i != far:
                    arrived(i).wait_recv()
                    onward(i).start()

        if far > 0:

            @pl.when(jnp.logical_and(is_stop, q == VIA - 2))
            def _():
                arrived(far).wait_recv()
                second_hop().start()

            @pl.when(jnp.logical_and(is_relay, q == VIA))
            def _():
                arrived(far).wait_recv()
                onward(far).start()

        for side in (LEFT, RIGHT):
            split_got(1, side, q)
            hacc[2 - 2 * side] += across(own_b[0, 1 - side, q], got_b[1, side, q])
            total[1 - side, q] = times(2 - 2 * side, 1, got_b[1, side, q])
        pl.when(q == 1)(lambda: reduce_sums(0))
        return carry

    lax.fori_loop(0, QUARTERS, third_step, 0)

    reduce_terms(1)
    finish_sums(0)

    def own_step(q, carry):
        for side in (LEFT, RIGHT):
            total[side, q] += times(1, 0, own_b[0, side, q])
        return carry

    lax.fori_loop(0, QUARTERS, own_step, 0)
    reduce_sums(1)

    def kernel_step(q, carry):
        for side in (LEFT, RIGHT):
            total[side, q] += times(1, 1, own_b[1, side, q])
        return carry

    lax.fori_loop(0, QUARTERS, kernel_step, 0)
    finish_sums(1)

    def take_last(side, q):
        if side == LEFT:
            if_comes(LEFT, lambda: take(send(0, LEFT, q)))
        else:
            around = jnp.logical_and(is_target, q == VIA)
            pl.when(around)(lambda: whole().wait_recv())
            pl.when(jnp.logical_and(has_before, jnp.logical_not(around)))(
                lambda: take(send(0, RIGHT, q))
            )

    def last_step(q, carry):
        sums = []
        for side in (LEFT, RIGHT):
            take_last(1 - side, q)
            split_got(0, 1 - side, q)
            sums.append(total[side, q] + times(2 * side, 0, got_b[0, 1 - side, q]))
        halves = [
            sums[side][:, t * 128 : (t + 1) * 128]
            for side in (LEFT, RIGHT)
            for t in range(TILES)
        ]
        for i, tile in enumerate(pick(halves, shift[...], lane)):
            at = pl.multiple_of(q * CHUNK_IN + i * 128, 128)
            out_ref[:, pl.ds(at, 128)] = tile
        return carry

    lax.fori_loop(0, QUARTERS, last_step, 0)

    @pl.when(is_relay)
    def _():
        for i in range(flows):
            onward(i).wait_send()

    if far > 0:
        pl.when(is_stop)(lambda: second_hop().wait_send())

    for group in range(2):
        for d in range(1, n_slab):
            spread(group, d).wait_send()
            share(group, d).wait_send()
    for q in range(QUARTERS):
        for m in range(2):
            if_goes(LEFT, lambda: drain(send(m, LEFT, q)))
            if (m, q) == (0, VIA):
                pl.when(is_source)(lambda: whole().wait_send())
                pl.when(jnp.logical_and(has_after, jnp.logical_not(is_source)))(
                    lambda: drain(send(m, RIGHT, q))
                )
            else:
                if_goes(RIGHT, lambda: drain(send(m, RIGHT, q)))


def per_device(n_orb, n_slab, orbitals, offsets, pairs, kernel):
    f32, b16 = jnp.float32, jnp.bfloat16
    dma = pltpu.SemaphoreType.DMA
    hbm = pl.BlockSpec(memory_space=pltpu.HBM)
    vmem = pl.BlockSpec(memory_space=pltpu.VMEM)
    operands = (orbitals, offsets.reshape(n_orb, BLOCK), pairs, kernel)

    def call(most, number):
        return pl.pallas_call(
            functools.partial(body, n_orb, n_slab, most),
            out_shape=(
                pltpu.VMEM((BLOCK, QUARTERS * CHUNK_IN), f32),
                pltpu.VMEM((8, 128), jnp.int32),
            ),
            in_specs=[hbm] * 4,
            out_specs=(vmem, vmem),
            scratch_shapes=[
                pltpu.VMEM((n_orb, BLOCK), jnp.int32),
                pltpu.VMEM(pairs.shape, jnp.int32),
                pltpu.VMEM(kernel.shape, f32),
                pltpu.VMEM((2, QUARTERS, BLOCK, CHUNK_IN), f32),
                pltpu.VMEM((2, 2, QUARTERS, BLOCK, CHUNK), f32),
                pltpu.VMEM((2, 2, QUARTERS, BLOCK, CHUNK), f32),
                pltpu.VMEM((2, 2, QUARTERS, 2 * BLOCK, CHUNK), b16),
                pltpu.VMEM((2, 2, QUARTERS, 2 * BLOCK, CHUNK), b16),
                pltpu.VMEM((BLOCK, BLOCK), jnp.int32),
                pltpu.VMEM((BLOCK, BLOCK), jnp.int32),
                pltpu.VMEM((3, BLOCK, 2 * BLOCK), b16),
                pltpu.VMEM((3, 2 * BLOCK, 2 * BLOCK), f32),
                pltpu.VMEM((3, BLOCK, BLOCK), f32),
                pltpu.VMEM((n_slab, 3, BLOCK // n_slab, BLOCK), f32),
                pltpu.VMEM((3, BLOCK, BLOCK), f32),
                pltpu.VMEM((3, 2, 2 * BLOCK, 2 * BLOCK), b16),
                pltpu.VMEM((2, QUARTERS, BLOCK, CHUNK), f32),
                dma((2, QUARTERS)), dma((2, 2, QUARTERS, 2)), dma((2, 2, QUARTERS, 2)),
                dma((2, n_slab)), dma((2, n_slab)), dma((2, n_slab)), dma((2, n_slab)),
                dma((3,)),
                pltpu.VMEM((n_orb // ROW - 1, BLOCK, CHUNK), f32),
                dma((n_orb // ROW - 1,)), dma((n_orb // ROW - 1,)),
                pltpu.SemaphoreType.REGULAR,
            ],
            compiler_params=pltpu.CompilerParams(
                collective_id=number, has_side_effects=True,
                vmem_limit_bytes=40 * 2**20,
            ),
            cost_estimate=pl.CostEstimate(
                flops=2400 * 10**6, bytes_accessed=4 * 2**20, transcendentals=0
            ),
        )(*(pltpu.with_memory_space_constraint(x, pltpu.HBM) for x in operands))

    result, over = call(MOST_ROWS, 0)
    return lax.cond(over[0, 0] > 0, lambda: call(BLOCK, 1)[0], lambda: result)


def solution(mesh):
    n_orb, n_slab = mesh.shape["orb"], mesh.shape["slab"]
    placed = (P(None, "orb", "slab"), P(), P("orb", None), P("orb", None, None, None))
    return jax.shard_map(
        functools.partial(per_device, n_orb, n_slab), mesh=mesh, in_specs=placed,
        out_specs=P("orb", "slab"), check_vma=False,
    )
```

time: 43.3 us -> 42.1 us (0.972)
  Pallas kernels: 42.1 us -> 39.8 us
  between operations: 0.01 us -> 0.67 us
  local copies, waits for them, and re-layouts: 0.97 us -> 1.49 us
    pallas_call x1, Pallas kernels: 42.1 us -> 39.8 us  [call(): pl.pallas_call(functools.partial(body, n_orb, n_slab, most), out_shape=(p...]
    slice x0 -> x1, local copies, waits for them, and re-layouts: none -> 0.51 us  [per_device(): return lax.cond(over[0, 0] > 0, lambda: call(BLOCK, 1)[0], lambda: result)]
where the time goes in v4:
time: 42.1 us; the launch traced here: 41.9 us
  Pallas kernels  39.8 us (95%)
  local copies, waits for them, and re-layouts  1.49 us (4%)
  between operations  0.67 us (2%)
    pallas_call x1, Pallas kernels, call(): pl.pallas_call(functools.partial(body, n_orb, n_slab, most), out_shape=(p...  39.8 us
    unnamed x1, local copies, waits for them, and re-layouts  0.97 us

profile of v4, /device:TPU:25, one launch (start us, length us, event | category | flops | bytes accessed | tf_op | source)
XLA Modules:
  0.0 41.9 jit_solution(10050923428342521765)
XLA Ops:
  0.0 39.8 %shard_map.48 = (f32[128,2048]{1,0:T(8,128)S(1)}, s32[8,128]{1,0:T(8,128)S(1)}) custom-call(f32[2,128,2048]{2,1,0:T(8,128)} %orb_hbm.1, s32[32,128]{1,0:T(8,128)} %bitcast.2, s32[1,3]{1,0:T(1,128)} %pairs_hbm.1, f32[1,3,128,128]{3,2,1,0:T(8,128)} %ker_hbm.1), custom_call_target="tpu_custom_call" | custom-call | flops 2400000000 | bytes 4194304 | tf_op jit(solution)/shard_map/pallas_call | solution.py:561
  39.8 0.5 %slice.3 = s32[1,1]{1,0:T(1,128)} slice(s32[8,128]{1,0:T(8,128)S(1)} %get-tuple-element.24), slice={[0:1], [0:1]} | slice | bytes 8 | tf_op jit(solution)/shard_map/slice | solution.py:604
  40.9 1.0 %copy.10 = f32[128,2048]{1,0:T(8,128)} copy(f32[128,2048]{1,0:T(8,128)S(1)} %get-tuple-element.26) | data formatting | bytes 2097152
  (1 shorter events, 0.0 us)

commit v5 on v4

--- a/solution.py
+++ b/solution.py
@@ -331,9 +331,7 @@
     for inside in (windows < TILE, windows > SPREAD - TILE):
         count = jnp.sum(inside.astype(jnp.float32), axis=1, keepdims=True)
         excess = jnp.maximum(excess, count - most)
-    over_ref[...] = jnp.broadcast_to(
-        jnp.max(excess, axis=0, keepdims=True), (8, 128)
-    ).astype(jnp.int32)
+    over_ref[0, 0] = jnp.max(excess).astype(jnp.int32)
 
     lax.fori_loop(0, QUARTERS, blank, 0)
     other_sorters()
@@ -562,10 +560,10 @@
             functools.partial(body, n_orb, n_slab, most),
             out_shape=(
                 pltpu.VMEM((BLOCK, QUARTERS * CHUNK_IN), f32),
-                pltpu.VMEM((8, 128), jnp.int32),
+                pltpu.SMEM((1, 1), jnp.int32),
             ),
             in_specs=[hbm] * 4,
-            out_specs=(vmem, vmem),
+            out_specs=(vmem, pl.BlockSpec(memory_space=pltpu.SMEM)),
             scratch_shapes=[
                 pltpu.VMEM((n_orb, BLOCK), jnp.int32),
                 pltpu.VMEM(pairs.shape, jnp.int32),
@@ -601,7 +599,7 @@
         )(*(pltpu.with_memory_space_constraint(x, pltpu.HBM) for x in operands))
 
     result, over = call(MOST_ROWS, 0)
-    return lax.cond(over[0, 0] > 0, lambda: call(BLOCK, 1)[0], lambda: result)
+    return lax.cond(over.reshape(()) > 0, lambda: call(BLOCK, 1)[0], lambda: result)
 
 
 def solution(mesh):

time: 42.1 us -> 40.9 us (0.971)
  between operations: 0.67 us -> 0.02 us
  local copies, waits for them, and re-layouts: 1.49 us -> 0.97 us
    slice x1 -> x0, local copies, waits for them, and re-layouts: 0.51 us -> none  [per_device(): return lax.cond(over[0, 0] > 0, lambda: call(BLOCK, 1)[0], lambda: result)]
where the time goes in v5:
time: 40.9 us; the launch traced here: 40.8 us
  Pallas kernels  39.8 us (97%)
  local copies, waits for them, and re-layouts  0.97 us (2%)
    pallas_call x1, Pallas kernels, call(): pl.pallas_call(functools.partial(body, n_orb, n_slab, most), out_shape=(p...  39.8 us
    unnamed x1, local copies, waits for them, and re-layouts  0.97 us

profile of v5, /device:TPU:25, one launch (start us, length us, event | category | flops | bytes accessed | tf_op | source)
XLA Modules:
  0.0 40.8 jit_solution(15188776730211956558)
XLA Ops:
  0.0 39.8 %shard_map.48 = (f32[128,2048]{1,0:T(8,128)S(1)}, s32[1,1]{1,0:T(1,128)S(4)}) custom-call(f32[2,128,2048]{2,1,0:T(8,128)} %orb_hbm.1, s32[32,128]{1,0:T(8,128)} %bitcast.2, s32[1,3]{1,0:T(1,128)} %pairs_hbm.1, f32[1,3,128,128]{3,2,1,0:T(8,128)} %ker_hbm.1), custom_call_target="tpu_custom_call" | custom-call | flops 2400000000 | bytes 4194304 | tf_op jit(solution)/shard_map/pallas_call | solution.py:559
  39.8 1.0 %copy.10 = f32[128,2048]{1,0:T(8,128)} copy(f32[128,2048]{1,0:T(8,128)S(1)} %get-tuple-element.26) | data formatting | bytes 2097152
  (1 shorter events, 0.0 us)

commit v6 on v5

--- a/solution.py
+++ b/solution.py
@@ -91,7 +91,7 @@
     n_orb, n_slab, most, orb_hbm, off_hbm, pairs_hbm, ker_hbm, out_ref, over_ref,
     off_ref, pairs_ref, ker_ref, x_in, own, got, own_b, got_b, shift, sorted_shift, sorter, hacc, hpart, hin, hsum, mats, total,
     in_sem, send_sem, recv_sem, rs_send, rs_recv, ag_send, ag_recv, small_sem,
-    held, held_sem, onward_sem, ready_sem,
+    held, held_sem, onward_sem, ready_sem, peers_sem,
 ):
     me = lax.axis_index("orb")
     mine = lax.axis_index("slab")
@@ -209,7 +209,7 @@
     pl.when(is_target)(lambda: greet((last, mine)))
     for d in range(1, n_slab):
         peer = lax.rem(mine + d, n_slab)
-        greet((me, peer))
+        pl.when(peer > mine)(lambda: greet((me, peer)))
     for q in range(1, QUARTERS):
         load(1, q).start()
     for q in range(QUARTERS):
@@ -265,7 +265,7 @@
     place_chunk(1, 0)
     pl.semaphore_wait(
         barrier,
-        n_slab - 1 + has_before.astype(jnp.int32) + has_after.astype(jnp.int32)
+        mine + has_before.astype(jnp.int32) + has_after.astype(jnp.int32)
         + (2 * flows - (far > 0)) * is_relay.astype(jnp.int32)
         + is_stop.astype(jnp.int32),
     )
@@ -286,6 +286,15 @@
         pl.when(is_stop)(lambda: ready(far))
 
     send_both(1, 0)
+
+    for d in range(1, n_slab):
+        peer = lax.rem(mine + d, n_slab)
+
+        @pl.when(peer < mine)
+        def _():
+            pl.semaphore_signal(
+                peers_sem, inc=1, device_id=(me, peer), device_id_type=MESH
+            )
 
     def first_step(q, carry):
         load(1, q).wait()
@@ -428,6 +437,9 @@
     def times(k, m, stack):
         return fold(jnp.dot(mats[k, m], stack, preferred_element_type=jnp.float32))
 
+    pl.when(mine < n_slab - 1)(
+        lambda: pl.semaphore_wait(peers_sem, n_slab - 1 - mine)
+    )
     reduce_terms(0)
 
     @pl.when(is_source)
@@ -587,7 +599,7 @@
                 dma((3,)),
                 pltpu.VMEM((n_orb // ROW - 1, BLOCK, CHUNK), f32),
                 dma((n_orb // ROW - 1,)), dma((n_orb // ROW - 1,)),
-                pltpu.SemaphoreType.REGULAR,
+                pltpu.SemaphoreType.REGULAR, pltpu.SemaphoreType.REGULAR,
             ],
             compiler_params=pltpu.CompilerParams(
                 collective_id=number, has_side_effects=True,

time: 40.9 us -> 40.2 us (0.983)
  Pallas kernels: 39.8 us -> 39 us
    pallas_call x1, Pallas kernels: 39.8 us -> 39 us  [call(): pl.pallas_call(functools.partial(body, n_orb, n_slab, most), out_shape=(p...]
where the time goes in v6:
time: 40.2 us; the launch traced here: 40 us
  Pallas kernels  39 us (97%)
  local copies, waits for them, and re-layouts  0.97 us (2%)
    pallas_call x1, Pallas kernels, call(): pl.pallas_call(functools.partial(body, n_orb, n_slab, most), out_shape=(p...  39 us
    unnamed x1, local copies, waits for them, and re-layouts  0.97 us

profile of v6, /device:TPU:25, one launch (start us, length us, event | category | flops | bytes accessed | tf_op | source)
XLA Modules:
  0.0 40.0 jit_solution(5300785123108048889)
XLA Ops:
  0.0 39.0 %shard_map.48 = (f32[128,2048]{1,0:T(8,128)S(1)}, s32[1,1]{1,0:T(1,128)S(4)}) custom-call(f32[2,128,2048]{2,1,0:T(8,128)} %orb_hbm.1, s32[32,128]{1,0:T(8,128)} %bitcast.2, s32[1,3]{1,0:T(1,128)} %pairs_hbm.1, f32[1,3,128,128]{3,2,1,0:T(8,128)} %ker_hbm.1), custom_call_target="tpu_custom_call" | custom-call | flops 2400000000 | bytes 4194304 | tf_op jit(solution)/shard_map/pallas_call | solution.py:571
  39.0 1.0 %copy.10 = f32[128,2048]{1,0:T(8,128)} copy(f32[128,2048]{1,0:T(8,128)S(1)} %get-tuple-element.26) | data formatting | bytes 2097152
  (1 shorter events, 0.0 us)

commit v7 on v6

--- a/solution.py
+++ b/solution.py
@@ -23,7 +23,7 @@
 MESH = pl.DeviceIdType.MESH
 LEFT, RIGHT = 0, 1
 ROW = 8
-VIA = QUARTERS - 1
+VIA = QUARTERS - 2
 
 
 def lane_gather(tile, index):
@@ -453,13 +453,13 @@
         got_b[m, side, q, BLOCK:, :] = low
 
     def third_step(q, carry):
-        for side in (LEFT, RIGHT):
-            if_comes(side, lambda: take(send(1, side, q)))
         if_goes(LEFT, lambda: start(send(0, LEFT, q)))
         straight = jnp.logical_not(jnp.logical_and(is_source, q == VIA))
         pl.when(jnp.logical_and(has_after, straight))(
             lambda: start(send(0, RIGHT, q))
         )
+        for side in (LEFT, RIGHT):
+            if_comes(side, lambda: take(send(1, side, q)))
 
         @pl.when(jnp.logical_and(is_relay, q == VIA - 1))
         def _():

time: 40.2 us -> 40.2 us (level)
  no operation moved by 1% of the time
where the time goes in v7:
time: 40.2 us; the launch traced here: 40 us
  Pallas kernels  39 us (97%)
  local copies, waits for them, and re-layouts  0.97 us (2%)
    pallas_call x1, Pallas kernels, call(): pl.pallas_call(functools.partial(body, n_orb, n_slab, most), out_shape=(p...  39 us
    unnamed x1, local copies, waits for them, and re-layouts  0.97 us

profile of v7, /device:TPU:25, one launch (start us, length us, event | category | flops | bytes accessed | tf_op | source)
XLA Modules:
  0.0 40.0 jit_solution(8227089625560799857)
XLA Ops:
  0.0 39.0 %shard_map.48 = (f32[128,2048]{1,0:T(8,128)S(1)}, s32[1,1]{1,0:T(1,128)S(4)}) custom-call(f32[2,128,2048]{2,1,0:T(8,128)} %orb_hbm.1, s32[32,128]{1,0:T(8,128)} %bitcast.2, s32[1,3]{1,0:T(1,128)} %pairs_hbm.1, f32[1,3,128,128]{3,2,1,0:T(8,128)} %ker_hbm.1), custom_call_target="tpu_custom_call" | custom-call | flops 2400000000 | bytes 4194304 | tf_op jit(solution)/shard_map/pallas_call | solution.py:571
  39.1 1.0 %copy.10 = f32[128,2048]{1,0:T(8,128)} copy(f32[128,2048]{1,0:T(8,128)S(1)} %get-tuple-element.26) | data formatting | bytes 2097152
  (1 shorter events, 0.0 us)

commit v8 on v6

--- a/solution.py
+++ b/solution.py
@@ -237,8 +237,10 @@
     one_hot = sorter_of(across_lanes, down_rows)
     sorter[1, :, :BLOCK] = one_hot.astype(jnp.bfloat16)
     sorter[1, :, BLOCK:] = one_hot.astype(jnp.bfloat16)
-    sorted_rows = jnp.sum(one_hot * across_lanes.astype(jnp.float32), axis=1, keepdims=True)
-    sorted_shift[...] = jnp.broadcast_to(sorted_rows, (BLOCK, BLOCK)).astype(jnp.int32)
+    sorted_shift[...] = jnp.dot(
+        sorter[1, :, :BLOCK], down_rows.astype(jnp.float32).astype(jnp.bfloat16),
+        preferred_element_type=jnp.float32,
+    ).astype(jnp.int32)
 
     def place_chunk(m, q):
         high, low = split_rows(x_in[m, q])

time: 40.2 us -> 40.2 us (level)
  no operation moved by 1% of the time
where the time goes in v8:
time: 40.2 us; the launch traced here: 40 us
  Pallas kernels  39 us (97%)
  local copies, waits for them, and re-layouts  0.97 us (2%)
    pallas_call x1, Pallas kernels, call(): pl.pallas_call(functools.partial(body, n_orb, n_slab, most), out_shape=(p...  39 us
    unnamed x1, local copies, waits for them, and re-layouts  0.97 us

profile of v8, /device:TPU:25, one launch (start us, length us, event | category | flops | bytes accessed | tf_op | source)
XLA Modules:
  0.0 40.0 jit_solution(14581131229603611863)
XLA Ops:
  0.0 39.0 %shard_map.48 = (f32[128,2048]{1,0:T(8,128)S(1)}, s32[1,1]{1,0:T(1,128)S(4)}) custom-call(f32[2,128,2048]{2,1,0:T(8,128)} %orb_hbm.1, s32[32,128]{1,0:T(8,128)} %bitcast.2, s32[1,3]{1,0:T(1,128)} %pairs_hbm.1, f32[1,3,128,128]{3,2,1,0:T(8,128)} %ker_hbm.1), custom_call_target="tpu_custom_call" | custom-call | flops 2400000000 | bytes 4194304 | tf_op jit(solution)/shard_map/pallas_call | solution.py:573
  39.1 1.0 %copy.10 = f32[128,2048]{1,0:T(8,128)} copy(f32[128,2048]{1,0:T(8,128)S(1)} %get-tuple-element.26) | data formatting | bytes 2097152
  (1 shorter events, 0.0 us)
